TPU v7x, 32 devices: a whole 2x2x4 slice. The times are simulated.
32 devices in a mesh: dp: 4 (over y, x), shard: 8 (over z, core).
Axes of the slice: x: 2, y: 2, z: 4, core: 2. Of those that a mesh axis runs over, the one named last changes fastest.
Arguments:
- hot_ids: int32 [4096, 8], P(('dp', 'shard')), may hold values from 0 to 4095
- cold_owner: int32 [8192, 1], P(('dp', 'shard')), may hold values from 0 to 7; in each aligned block of 256 rows (0 to 255, 256 to 511, ...) at most 64 rows name the same one
- cold_offset: int32 [8192], P(('dp', 'shard')), may hold values from 0 to 4095
- hot_table: bfloat16 [4096, 128], replicated, may hold values from -2 to 2
- cold_table: bfloat16 [32768, 128], P('shard'), may hold values from -4 to 4
- w_in: bfloat16 [256, 4096], P(None, 'shard'), may hold values from -0.375 to 0.375
- bias_in: bfloat16 [1, 4096], P(None, 'shard'), may hold values from -0.59765625 to 0.59765625
- w_out: bfloat16 [1, 4096], P(None, 'shard'), may hold values from -0.1875 to 0.1875
- cotangent: float32 [4096], P(('dp', 'shard')), may hold values from -10 to 10
Outputs:
- logits: float32 [4096], P(('dp', 'shard'))
- hot_grad: bfloat16 [4096, 128], P('shard')
- cold_grad: bfloat16 [32768, 128], P('shard')
- w_in_grad: float32 [256, 4096], P(None, 'shard')
Inputs may be any that keep to these rules, and one draw needn't show every extreme that they name: `cold_owner`: within the 256 cold lookups of one device no owner is named more than 64 times, a bound that some block reaches.
All inputs are finite; a program needn't handle non-finite values.
Results may differ from a plain program's by a relative error of at most 0.015.
Values may be sent and summed in bfloat16 or wider, within the bound.
A program may use at most 64 MiB of HBM per device.

v0:
```python
import jax
import jax.numpy as jnp
from jax import lax
from jax.sharding import PartitionSpec as P


def contract_rows(left, right):
    return lax.dot_general(
        left, right, (((0,), (0,)), ((), ())), preferred_element_type=jnp.float32
    )


def shards(
    hot_ids, cold_owner, cold_offset, hot_table, cold_table, w_in, bias_in, w_out, cotangent
):
    shard_count = lax.axis_size("shard")
    my_index = lax.axis_index("shard")
    samples_dev = hot_ids.shape[0]
    hot_width = hot_ids.shape[1]
    table_rows = hot_table.shape[0]
    embed = hot_table.shape[1]
    kept_rows = table_rows // shard_count
    owned_rows = cold_table.shape[0]
    row_numbers = jnp.arange(table_rows, dtype=jnp.int32)
    hot_counts = jnp.zeros((samples_dev, table_rows), jnp.float32)
    for lookup in range(hot_width):
        hot_counts = hot_counts + (hot_ids[:, lookup][:, None] == row_numbers[None, :]).astype(
            jnp.float32
        )
    hot_counts = hot_counts.astype(jnp.bfloat16)
    hot_pooled = jnp.dot(hot_counts, hot_table, preferred_element_type=jnp.float32)
    owner_ids = cold_owner[:, 0]
    lookups = owner_ids.shape[0]
    per_sample = lookups // samples_dev
    capacity = max(2, 2 * lookups // shard_count)
    matches = (owner_ids[:, None] == jnp.arange(shard_count, dtype=jnp.int32)[None, :]).astype(
        jnp.int32
    )
    ordinal = jnp.cumsum(matches, axis=0) - 1
    slot_index = jnp.sum(ordinal * matches, axis=1)
    slot_place = owner_ids * capacity + slot_index
    slot_match = slot_place[:, None] == jnp.arange(shard_count * capacity, dtype=jnp.int32)[None, :]
    requests = jnp.sum(jnp.where(slot_match, cold_offset[:, None], 0), axis=0).reshape(
        shard_count, capacity
    )
    present = jnp.sum(slot_match.astype(jnp.int32), axis=0).reshape(shard_count, capacity)
    slot_table = slot_match.astype(jnp.bfloat16)
    offsets = lax.all_to_all(requests, "shard", split_axis=0, concat_axis=0, tiled=True)
    markers = lax.all_to_all(present, "shard", split_axis=0, concat_axis=0, tiled=True)
    fetched = jnp.take(cold_table, offsets, axis=0)
    fetched = jnp.where(markers[:, :, None] > 0, fetched, jnp.zeros_like(fetched))
    answer = lax.all_to_all(fetched, "shard", split_axis=0, concat_axis=0, tiled=True)
    mine = jnp.dot(slot_table, answer.reshape(-1, embed), preferred_element_type=jnp.float32)
    cold_pooled = jnp.sum(mine.reshape(samples_dev, per_sample, embed), axis=1)
    inputs = jnp.concatenate([hot_pooled, cold_pooled], axis=1).astype(jnp.bfloat16)
    group_inputs = lax.all_gather(inputs, "shard", axis=0, tiled=True)
    preact = (
        jnp.dot(group_inputs, w_in, preferred_element_type=jnp.float32)
        + bias_in[0].astype(jnp.float32)[None, :]
    )
    sigma = jax.nn.sigmoid(preact)
    hidden = (preact * sigma).astype(jnp.bfloat16)
    logit_share = jnp.dot(hidden, w_out[0], preferred_element_type=jnp.float32)
    group_logits = lax.psum(logit_share, "shard")
    logits = lax.dynamic_slice_in_dim(group_logits, my_index * samples_dev, samples_dev, 0)
    group_cotangent = lax.all_gather(cotangent, "shard", axis=0, tiled=True)
    slope = sigma * (1.0 + preact * (1.0 - sigma))
    hidden_grad = (group_cotangent[:, None] * w_out[0].astype(jnp.float32)[None, :] * slope).astype(
        jnp.bfloat16
    )
    weight_group = contract_rows(group_inputs, hidden_grad).astype(jnp.bfloat16)
    input_grad = lax.psum_scatter(
        jnp.dot(hidden_grad, w_in.T, preferred_element_type=jnp.float32).astype(jnp.bfloat16),
        "shard",
        scatter_dimension=0,
        tiled=True,
    )
    hot_part = contract_rows(hot_counts, input_grad[:, :embed])
    hot_everywhere = lax.psum(hot_part, ("dp", "shard"))
    hot_total = lax.dynamic_slice_in_dim(hot_everywhere, my_index * kept_rows, kept_rows, 0)
    per_lookup = jnp.repeat(input_grad[:, embed:], per_sample, axis=0)
    outgoing = (
        contract_rows(slot_table, per_lookup)
        .astype(jnp.bfloat16)
        .reshape(shard_count, capacity, embed)
    )
    incoming = lax.all_to_all(outgoing, "shard", split_axis=0, concat_axis=0, tiled=True)
    offset_table = (
        offsets.reshape(-1)[:, None] == jnp.arange(owned_rows, dtype=jnp.int32)[None, :]
    ).astype(jnp.bfloat16)
    cold_part = contract_rows(offset_table, incoming.reshape(-1, embed))
    cold_total, weight_total = (
        lax.psum(cold_part.astype(jnp.bfloat16), "dp").astype(jnp.float32),
        lax.psum(weight_group, "dp").astype(jnp.float32),
    )
    return (logits, hot_total.astype(jnp.bfloat16), cold_total.astype(jnp.bfloat16), weight_total)


def solution(mesh):
    in_specs = (
        P(("dp", "shard"), None),
        P(("dp", "shard"), None),
        P(("dp", "shard")),
        P(),
        P("shard", None),
        P(None, "shard"),
        P(None, "shard"),
        P(None, "shard"),
        P(("dp", "shard")),
    )
    out_specs = (P(("dp", "shard")), P("shard", None), P("shard", None), P(None, "shard"))
    return jax.shard_map(shards, mesh=mesh, in_specs=in_specs, out_specs=out_specs, check_vma=False)
```

profile of v0, /device:TPU:0, one launch (start us, length us, event | category | flops | bytes accessed | tf_op | source)
XLA Modules:
  0.0 214.7 jit_solution(14971163135114629105)
XLA Ops:
  10.1 1.3 fusion.14
  12.9 6.3 %all-to-all-start.1 = ((s32[8,1,64]{2,1,0:T(1,128)}), s32[8,1,64]{2,1,0:T(1,128)S(1)}, u32[]{:S(2)}, u32[]{:S(2)}) async-start(s32[8,1,64]{2,1,0:T(1,128)} %all_to_all.24), calls=%async_computation.1 | async-start | bytes 8192 | tf_op jit(solution)/shard_map/all_to_all | solution.py:48
  22.5 12.3 %all-gather = f32[8,1,128]{2,1,0:T(1,128)S(1)} all-gather(f32[1,1,128]{2,1,0:T(1,128)} %bitcast.77), channel_id=1, replica_groups=mesh['dp'=4,'shard'=8] {'shard'}, dimensions={0}, use_global_device_ids=true | all-gather | bytes 4608 | tf_op jit(solution)/shard_map/all_gather | solution.py:66
  34.8 3.3 %all-to-all-start = ((s32[8,1,64]{2,1,0:T(1,128)}), s32[8,1,64]{2,1,0:T(1,128)S(1)}, u32[]{:S(2)}, u32[]{:S(2)}) async-start(s32[8,1,64]{2,1,0:T(1,128)} %all_to_all.22), calls=%async_computation | async-start | bytes 8192 | tf_op jit(solution)/shard_map/all_to_all | solution.py:49
  38.3 5.3 %all-to-all-done = s32[8,1,64]{2,1,0:T(1,128)S(1)} async-done(((s32[8,1,64]{2,1,0:T(1,128)}), s32[8,1,64]{2,1,0:T(1,128)S(1)}, u32[]{:S(2)}, u32[]{:S(2)}) %all-to-all-start) | async-done | bytes 2080 | tf_op jit(solution)/shard_map/all_to_all | solution.py:49
  43.6 1.3 gather_fusion
  45.8 3.4 %all-to-all-start.2 = ((bf16[8,64,128]{2,1,0:T(8,128)(2,1)}), bf16[8,64,128]{2,1,0:T(8,128)(2,1)S(1)}, u32[]{:S(2)}, u32[]{:S(2)}) async-start(bf16[8,64,128]{2,1,0:T(8,128)(2,1)} %select_select_fusion), calls=%async_computation.2 | async-start | bytes 262144 | tf_op jit(solution)/shard_map/all_to_all | solution.py:52
  49.2 3.7 %convolution_convert_fusion.3 = bf16[128,128]{0,1:T(8,128)(2,1)S(1)} fusion(bf16[4096,128]{1,0:T(8,128)(2,1)} %param.12, s32[128]{0:T(128)S(1)} %get-tuple-element.16, s32[128]{0:T(128)S(1)} %get-tuple-element.17, s32[128]{0:T(128)S(1)} %get-tuple-element.11, s32[128]{0:T(128)S(1)} %get-tuple-element.12, s32[128]{0:T(128)S(1)} %get-tuple-element.13, ...), kind=kOutput, calls=%fused_computation.21 | convolution fusion | flops 146817024 | bytes 1085440 | tf_op jit(solution)/shard_map/dot_general | solution.py:31
  53.0 2.9 %all-to-all-done.2 = bf16[8,64,128]{2,1,0:T(8,128)(2,1)S(1)} async-done(((bf16[8,64,128]{2,1,0:T(8,128)(2,1)}), bf16[8,64,128]{2,1,0:T(8,128)(2,1)S(1)}, u32[]{:S(2)}, u32[]{:S(2)}) %all-to-all-start.2) | async-done | bytes 131104 | tf_op jit(solution)/shard_map/all_to_all | solution.py:52
  56.3 14.0 %all_gather.6 = bf16[1024,256]{0,1:T(8,128)(2,1)S(1)} all-gather(bf16[128,256]{0,1:T(8,128)(2,1)S(1)} %pad_maximum_fusion), channel_id=1, replica_groups=mesh['dp'=4,'shard'=8] {'shard'}, dimensions={0}, use_global_device_ids=true | all-gather | bytes 589824 | tf_op jit(solution)/shard_map/all_gather | solution.py:56
  70.3 2.3 %multiply_convert_fusion = (bf16[1024,512]{1,0:T(8,128)(2,1)S(1)}, f32[1024,512]{1,0:T(8,128)}) fusion(f32[512]{0:T(512)S(1)} %mul.50, f32[1024]{0:T(1024)S(1)} %bitcast.70, f32[512]{0:T(512)S(1)} %bitcast.75, bf16[1024,256]{0,1:T(8,128)(2,1)S(1)} %all_gather.6, bf16[256,512]{1,0:T(8,128)(2,1)S(1)} %copy-done.1), kind=kOutput, calls=%fused_computation.5 | convolution fusion | flops 274202624 | bytes 3940352 | tf_op jit(solution)/shard_map/dot_general | solution.py:58
  72.6 1.3 convolution_convert_fusion
  74.6 28.9 %reduce-scatter.2.cloned.1.call-done = bf16[128,256]{1,0:T(8,128)(2,1)} async-done(((bf16[1024,256]{1,0:T(8,128)(2,1)}), bf16[128,256]{1,0:T(8,128)(2,1)}) %reduce-scatter.2.cloned.1.call-update) | async-done | bytes 65552 | tf_op jit(solution)/shard_map/reduce_scatter | solution.py:72
  105.4 3.4 %all-to-all-start.3 = ((bf16[8,64,128]{2,1,0:T(8,128)(2,1)}), bf16[8,64,128]{2,1,0:T(8,128)(2,1)S(1)}, u32[]{:S(2)}, u32[]{:S(2)}) async-start(bf16[8,64,128]{2,1,0:T(8,128)(2,1)} %bitcast.27), calls=%async_computation.4 | async-start | bytes 262144 | tf_op jit(solution)/shard_map/all_to_all | solution.py:87
  108.8 1.2 convolution_convert_fusion.1
  110.0 5.5 %all-to-all-done.3 = bf16[8,64,128]{2,1,0:T(8,128)(2,1)S(1)} async-done(((bf16[8,64,128]{2,1,0:T(8,128)(2,1)}), bf16[8,64,128]{2,1,0:T(8,128)(2,1)S(1)}, u32[]{:S(2)}, u32[]{:S(2)}) %all-to-all-start.3) | async-done | bytes 131104 | tf_op jit(solution)/shard_map/all_to_all | solution.py:87
  115.5 3.4 %fusion.1 = bf16[4096,128]{1,0:T(8,128)(2,1)} fusion(bf16[512,128]{1,0:T(8,128)(2,1)S(1)} %bitcast.62, s32[512]{0:T(512)S(1)} %eq.248), kind=kOutput, calls=%fused_computation.3 | convolution fusion | flops 539492352 | bytes 1181696 | tf_op jit(solution)/shard_map/dot_general | solution.py:8
  118.9 2.3 %fusion.3 = f32[1,1024]{1,0:T(1,128)S(1)} fusion(f32[1024,512]{1,0:T(8,128)} %get-tuple-element.19, f32[512]{0:T(512)S(1)} %bitcast.76, bf16[1,512]{1,0:T(2,128)(2,1)S(1)} %copy-done.3), kind=kOutput, calls=%fused_computation.22 | convolution fusion | flops 4194304 | bytes 2104320 | tf_op jit(solution)/shard_map/dot_general | solution.py:63
  121.2 14.4 %psum.28 = f32[1024]{0:T(1024)S(1)} all-reduce(f32[1024]{0:T(1024)S(1)} %bitcast.71), channel_id=1, replica_groups=mesh['dp'=4,'shard'=8] {'shard'}, use_global_device_ids=true, to_apply=%region_6.7 | all-reduce | flops 1024 | bytes 8192 | tf_op jit(solution)/shard_map/psum | solution.py:64
  136.2 2.3 %fusion.6 = f32[4096,128]{1,0:T(8,128)S(1)} fusion(s32[128]{0:T(128)S(1)} %get-tuple-element.16, s32[128]{0:T(128)S(1)} %get-tuple-element.17, s32[128]{0:T(128)S(1)} %get-tuple-element.11, s32[128]{0:T(128)S(1)} %get-tuple-element.12, s32[128]{0:T(128)S(1)} %get-tuple-element.13, s32[128]{0:T(128)S(1)} %get-tuple-element.14, ...), kind=kOutput, calls=%fused_computation.28 | convolution fusion | flops 146800640 | bytes 2134016 | tf_op jit(solution)/shard_map/dot_general | solution.py:8
  138.6 63.7 %all-reduce.5 = bf16[4096,128]{1,0:T(8,128)(2,1)} all-reduce(f32[4096,128]{1,0:T(8,128)S(1)} %fusion.6), channel_id=1, replica_groups=mesh['dp'=4,'shard'=8] {'dp','shard'}, use_global_device_ids=true, to_apply=%region_8.9 | all-reduce | flops 524288 | bytes 3145728 | tf_op jit(solution)/shard_map/psum | solution.py:79
  202.3 1.6 dynamic-slice_convert_fusion
  203.8 1.8 convert_element_type.86
  205.6 2.3 %copy.27 = bf16[4096,128]{1,0:T(8,128)(2,1)} copy(bf16[4096,128]{1,0:T(8,128)(2,1)} %get-tuple-element.22) | data formatting | bytes 2097152
  (45 shorter events, 12.4 us)
Async XLA Ops:
  7.2 36.4 %copy-start = (bf16[4096,128]{1,0:T(8,128)(2,1)S(1)}, bf16[4096,128]{1,0:T(8,128)(2,1)}, u32[]{:S(2)}) copy-start(bf16[4096,128]{1,0:T(8,128)(2,1)} %param.13) | copy-start | bytes 3145732
  12.9 21.9 %all-to-all-start.1 = ((s32[8,1,64]{2,1,0:T(1,128)}), s32[8,1,64]{2,1,0:T(1,128)S(1)}, u32[]{:S(2)}, u32[]{:S(2)}) async-start(s32[8,1,64]{2,1,0:T(1,128)} %all_to_all.24), calls=%async_computation.1 | async-start | bytes 8192 | tf_op jit(solution)/shard_map/all_to_all | solution.py:48
  34.8 8.7 %all-to-all-start = ((s32[8,1,64]{2,1,0:T(1,128)}), s32[8,1,64]{2,1,0:T(1,128)S(1)}, u32[]{:S(2)}, u32[]{:S(2)}) async-start(s32[8,1,64]{2,1,0:T(1,128)} %all_to_all.22), calls=%async_computation | async-start | bytes 8192 | tf_op jit(solution)/shard_map/all_to_all | solution.py:49
  45.8 10.1 %all-to-all-start.2 = ((bf16[8,64,128]{2,1,0:T(8,128)(2,1)}), bf16[8,64,128]{2,1,0:T(8,128)(2,1)S(1)}, u32[]{:S(2)}, u32[]{:S(2)}) async-start(bf16[8,64,128]{2,1,0:T(8,128)(2,1)} %select_select_fusion), calls=%async_computation.2 | async-start | bytes 262144 | tf_op jit(solution)/shard_map/all_to_all | solution.py:52
  49.2 54.3 %reduce-scatter.2.cloned.1.call-start = ((), (), s32[]{:S(2)}) async-start(), calls=%async_computation.5 | async-start | bytes 589824 | tf_op jit(solution)/shard_map/reduce_scatter | solution.py:72
  49.2 21.1 %copy-start.1 = (bf16[256,512]{1,0:T(8,128)(2,1)S(1)}, bf16[256,512]{1,0:T(8,128)(2,1)}, u32[]{:S(2)}) copy-start(bf16[256,512]{1,0:T(8,128)(2,1)} %param.14) | copy-start | bytes 786436
  105.4 10.1 %all-to-all-start.3 = ((bf16[8,64,128]{2,1,0:T(8,128)(2,1)}), bf16[8,64,128]{2,1,0:T(8,128)(2,1)S(1)}, u32[]{:S(2)}, u32[]{:S(2)}) async-start(bf16[8,64,128]{2,1,0:T(8,128)(2,1)} %bitcast.27), calls=%async_computation.4 | async-start | bytes 262144 | tf_op jit(solution)/shard_map/all_to_all | solution.py:87
  108.8 95.1 %all-reduce.4.cloned.1.call-start = ((), (), s32[]{:S(2)}) async-start(), calls=%async_computation.6 | async-start | bytes 2621440 | tf_op jit(solution)/shard_map/psum | solution.py:93
  115.5 3.4 %copy-start.3 = (bf16[1,512]{1,0:T(2,128)(2,1)S(1)}, bf16[1,512]{1,0:T(2,128)(2,1)}, u32[]{:S(2)}) copy-start(bf16[1,512]{1,0:T(2,128)(2,1)} %param.16) | copy-start | bytes 3076
  118.9 17.3 %copy-start.2 = (bf16[128,256]{1,0:T(8,128)(2,1)S(1)}, bf16[128,256]{1,0:T(8,128)(2,1)}, u32[]{:S(2)}) copy-start(bf16[128,256]{1,0:T(8,128)(2,1)} %reduce-scatter.2.cloned.1.call-done) | copy-start | bytes 196612
Sparse Core Ops, SparseCore 0:
  74.0 29.4 reduce-scatter.1
  119.0 61.0 all-reduce.3
where the time goes:
time: 216 us; the launch traced here: 215 us
  blocking collectives  104 us (48%)
  waiting for transfers between devices  42.6 us (20%)
  matrix products  17.9 us (8%)
  starting transfers between devices  16.5 us (8%)
  between operations  14.2 us (7%)
  local copies, waits for them, and re-layouts  10.1 us (5%)
  other arithmetic  9.09 us (4%)
    psum x1, blocking collectives, shards(): hot_everywhere = lax.psum(hot_part, ('dp', 'shard'))  63.7 us
    reduce_scatter x1, waiting for transfers between devices, shards(): lax.psum_scatter(jnp.dot(hidden_grad, w_in.T, preferred_element_type=jnp....  28.9 us
    psum x1, blocking collectives, shards(): group_logits = lax.psum(logit_share, 'shard')  14.4 us
    all_gather x1, blocking collectives, shards(): group_inputs = lax.all_gather(inputs, 'shard', axis=0, tiled=True)  14 us
    all_gather x1, blocking collectives, shards(): group_cotangent = lax.all_gather(cotangent, 'shard', axis=0, tiled=True)  12.3 us
    dot_general x4, matrix products, contract_rows(): lax.dot_general(left, right, (((0,), (0,)), ((), ())), preferred_element_...  8.01 us
    all_to_all x1, starting transfers between devices, shards(): lax.all_to_all(requests, 'shard', split_axis=0, concat_axis=0, tiled=True)  6.33 us
    all_to_all x1, waiting for transfers between devices, shards(): lax.all_to_all(outgoing, 'shard', split_axis=0, concat_axis=0, tiled=True)  5.5 us
  transfers between devices with their start and end apart: 6, of which 4 were waited for; matrix products, arithmetic and copies ran while one was open for 7% of the time, Pallas kernels for 0%

commit v1 on v0

--- a/solution.py
+++ b/solution.py
@@ -2,6 +2,18 @@
 import jax.numpy as jnp
 from jax import lax
 from jax.sharding import PartitionSpec as P
+
+
+def cut_along(x, dim, size):
+    shape = x.shape
+    blocks = x.reshape(*shape[:dim], size, shape[dim] // size, *shape[dim + 1 :])
+    return jnp.moveaxis(blocks, dim, 0)
+
+
+def in_order(blocks, dim):
+    blocks = jnp.moveaxis(blocks, 0, dim)
+    shape = blocks.shape
+    return blocks.reshape(*shape[:dim], shape[dim] * shape[dim + 1], *shape[dim + 2 :])
 
 
 def contract_rows(left, right):
@@ -84,7 +96,14 @@
         .astype(jnp.bfloat16)
         .reshape(shard_count, capacity, embed)
     )
-    incoming = lax.all_to_all(outgoing, "shard", split_axis=0, concat_axis=0, tiled=True)
+    count, position = (lax.axis_size("shard"), lax.axis_index("shard"))
+    parts = cut_along(outgoing, 0, count)
+    outs = [parts[position]]
+    for lap in range(1, count):
+        sent = parts[(position + lap) % count]
+        outs.append(lax.ppermute(sent, "shard", [(i, (i + lap) % count) for i in range(count)]))
+    parts = jnp.stack(outs)[(position - jnp.arange(count)) % count]
+    incoming = in_order(parts, 0)
     offset_table = (
         offsets.reshape(-1)[:, None] == jnp.arange(owned_rows, dtype=jnp.int32)[None, :]
     ).astype(jnp.bfloat16)

time: 216 us -> 221 us (1.023)
  waiting for transfers between devices: 42.6 us -> 46.5 us
  starting transfers between devices: 16.5 us -> 19.4 us
    ppermute x0 -> x7, waiting for transfers between devices: none -> 9.59 us  [shards(): lax.ppermute(sent, 'shard', [(i, (i + lap) % count) for i in range(count)])]
    ppermute x0 -> x7, starting transfers between devices: none -> 6.27 us  [shards(): lax.ppermute(sent, 'shard', [(i, (i + lap) % count) for i in range(count)])]
    all_to_all x1 -> x0, waiting for transfers between devices: 5.5 us -> none  [shards(): lax.all_to_all(outgoing, 'shard', split_axis=0, concat_axis=0, tiled=True)]
    all_to_all x1 -> x0, starting transfers between devices: 3.37 us -> none  [shards(): lax.all_to_all(outgoing, 'shard', split_axis=0, concat_axis=0, tiled=True)]
  transfers between devices with their start and end apart: 6 -> 12, of which waited for: 4 -> 5; matrix products, arithmetic and copies ran while one was open for 7% -> 7% of each run, Pallas kernels for 0% -> 0%
where the time goes in v1:
time: 221 us
  blocking collectives  103 us (47%)
  waiting for transfers between devices  46.5 us (21%)
  starting transfers between devices  19.4 us (9%)
  matrix products  17.1 us (8%)
  between operations  14.4 us (7%)
  local copies, waits for them, and re-layouts  10.8 us (5%)
  other arithmetic  9.11 us (4%)
    psum x1, blocking collectives, shards(): hot_everywhere = lax.psum(hot_part, ('dp', 'shard'))  62.8 us
    reduce_scatter x1, waiting for transfers between devices, shards(): lax.psum_scatter(jnp.dot(hidden_grad, w_in.T, preferred_element_type=jnp....  28.7 us
    psum x1, blocking collectives, shards(): group_logits = lax.psum(logit_share, 'shard')  14.1 us
    all_gather x1, blocking collectives, shards(): group_inputs = lax.all_gather(inputs, 'shard', axis=0, tiled=True)  14 us
    all_gather x1, blocking collectives, shards(): group_cotangent = lax.all_gather(cotangent, 'shard', axis=0, tiled=True)  12.3 us
    ppermute x7, waiting for transfers between devices, shards(): lax.ppermute(sent, 'shard', [(i, (i + lap) % count) for i in range(count)])  9.59 us
    dot_general x4, matrix products, contract_rows(): lax.dot_general(left, right, (((0,), (0,)), ((), ())), preferred_element_...  7.32 us
    all_to_all x1, starting transfers between devices, shards(): lax.all_to_all(requests, 'shard', split_axis=0, concat_axis=0, tiled=True)  6.33 us
  transfers between devices with their start and end apart: 12, of which 5 were waited for; matrix products, arithmetic and copies ran while one was open for 7% of the time, Pallas kernels for 0%

profile of v1, /device:TPU:0, one launch (start us, length us, event | category | flops | bytes accessed | tf_op | source)
XLA Modules:
  0.0 220.5 jit_solution(12789885536328002633)
XLA Ops:
  10.1 1.3 fusion.16
  12.9 6.3 %all-to-all-start.1 = ((s32[8,1,64]{2,1,0:T(1,128)}), s32[8,1,64]{2,1,0:T(1,128)S(1)}, u32[]{:S(2)}, u32[]{:S(2)}) async-start(s32[8,1,64]{2,1,0:T(1,128)} %all_to_all.21), calls=%async_computation.1 | async-start | bytes 8192 | tf_op jit(solution)/shard_map/all_to_all | solution.py:60
  22.5 12.3 %all-gather = f32[8,1,128]{2,1,0:T(1,128)S(1)} all-gather(f32[1,1,128]{2,1,0:T(1,128)} %bitcast.110), channel_id=1, replica_groups=mesh['dp'=4,'shard'=8] {'shard'}, dimensions={0}, use_global_device_ids=true | all-gather | bytes 4608 | tf_op jit(solution)/shard_map/all_gather | solution.py:78
  34.8 3.3 %all-to-all-start = ((s32[8,1,64]{2,1,0:T(1,128)}), s32[8,1,64]{2,1,0:T(1,128)S(1)}, u32[]{:S(2)}, u32[]{:S(2)}) async-start(s32[8,1,64]{2,1,0:T(1,128)} %all_to_all.19), calls=%async_computation | async-start | bytes 8192 | tf_op jit(solution)/shard_map/all_to_all | solution.py:61
  38.3 5.3 %all-to-all-done = s32[8,1,64]{2,1,0:T(1,128)S(1)} async-done(((s32[8,1,64]{2,1,0:T(1,128)}), s32[8,1,64]{2,1,0:T(1,128)S(1)}, u32[]{:S(2)}, u32[]{:S(2)}) %all-to-all-start) | async-done | bytes 2080 | tf_op jit(solution)/shard_map/all_to_all | solution.py:61
  43.6 1.3 gather_fusion
  45.8 3.4 %all-to-all-start.2 = ((bf16[8,64,128]{2,1,0:T(8,128)(2,1)}), bf16[8,64,128]{2,1,0:T(8,128)(2,1)S(1)}, u32[]{:S(2)}, u32[]{:S(2)}) async-start(bf16[8,64,128]{2,1,0:T(8,128)(2,1)} %select_select_fusion), calls=%async_computation.2 | async-start | bytes 262144 | tf_op jit(solution)/shard_map/all_to_all | solution.py:64
  49.2 3.7 %convolution_convert_fusion.3 = bf16[128,128]{0,1:T(8,128)(2,1)S(1)} fusion(bf16[4096,128]{1,0:T(8,128)(2,1)} %param.12, s32[128]{0:T(128)S(1)} %get-tuple-element.24, s32[128]{0:T(128)S(1)} %get-tuple-element.25, s32[128]{0:T(128)S(1)} %get-tuple-element.19, s32[128]{0:T(128)S(1)} %get-tuple-element.20, s32[128]{0:T(128)S(1)} %get-tuple-element.21, ...), kind=kOutput, calls=%fused_computation.22 | convolution fusion | flops 146817024 | bytes 1085440 | tf_op jit(solution)/shard_map/dot_general | solution.py:43
  53.0 2.9 %all-to-all-done.2 = bf16[8,64,128]{2,1,0:T(8,128)(2,1)S(1)} async-done(((bf16[8,64,128]{2,1,0:T(8,128)(2,1)}), bf16[8,64,128]{2,1,0:T(8,128)(2,1)S(1)}, u32[]{:S(2)}, u32[]{:S(2)}) %all-to-all-start.2) | async-done | bytes 131104 | tf_op jit(solution)/shard_map/all_to_all | solution.py:64
  56.3 14.0 %all_gather.6 = bf16[1024,256]{0,1:T(8,128)(2,1)S(1)} all-gather(bf16[128,256]{0,1:T(8,128)(2,1)S(1)} %pad_maximum_fusion), channel_id=1, replica_groups=mesh['dp'=4,'shard'=8] {'shard'}, dimensions={0}, use_global_device_ids=true | all-gather | bytes 589824 | tf_op jit(solution)/shard_map/all_gather | solution.py:68
  70.3 2.3 %multiply_convert_fusion = (bf16[1024,512]{1,0:T(8,128)(2,1)S(1)}, f32[1024,512]{1,0:T(8,128)}) fusion(f32[512]{0:T(512)S(1)} %mul.50, f32[1024]{0:T(1024)S(1)} %bitcast.103, f32[512]{0:T(512)S(1)} %bitcast.108, bf16[1024,256]{0,1:T(8,128)(2,1)S(1)} %all_gather.6, bf16[256,512]{1,0:T(8,128)(2,1)S(1)} %copy-done.1), kind=kOutput, calls=%fused_computation.6 | convolution fusion | flops 274202624 | bytes 3940352 | tf_op jit(solution)/shard_map/dot_general | solution.py:70
  74.8 28.7 %reduce-scatter.2.cloned.1.call-done = bf16[128,256]{1,0:T(8,128)(2,1)} async-done(((bf16[1024,256]{1,0:T(8,128)(2,1)}), bf16[128,256]{1,0:T(8,128)(2,1)}) %reduce-scatter.2.cloned.1.call-update) | async-done | bytes 65552 | tf_op jit(solution)/shard_map/reduce_scatter | solution.py:84
  105.9 3.5 %collective-permute-start.6 = (bf16[1,64,128]{2,1,0:T(8,128)(2,1)S(1)}, bf16[1,64,128]{2,1,0:T(8,128)(2,1)S(1)}, u32[]{:S(2)}, u32[]{:S(2)}) collective-permute-start(bf16[1,64,128]{2,1,0:T(8,128)(2,1)S(1)} %get-tuple-element.10), channel_id=1, source_target_pairs={{0,7},{1,0},{2,1},{3,2},{4,3},{5,4},{6,5},{7,6},{8,15},{9,8},{10,9... | collective-permute-start | bytes 49160 | tf_op jit(solution)/shard_map/ppermute | solution.py:104
  109.5 2.7 %collective-permute-start.3 = (bf16[1,64,128]{2,1,0:T(8,128)(2,1)S(1)}, bf16[1,64,128]{2,1,0:T(8,128)(2,1)S(1)}, u32[]{:S(2)}, u32[]{:S(2)}) collective-permute-start(bf16[1,64,128]{2,1,0:T(8,128)(2,1)S(1)} %get-tuple-element.13), channel_id=1, source_target_pairs={{0,4},{1,5},{2,6},{3,7},{4,0},{5,1},{6,2},{7,3},{8,12},{9,13},{10,... | collective-permute-start | bytes 49160 | tf_op jit(solution)/shard_map/ppermute | solution.py:104
  112.1 5.5 %collective-permute-done.1 = bf16[1,64,128]{2,1,0:T(8,128)(2,1)S(1)} collective-permute-done((bf16[1,64,128]{2,1,0:T(8,128)(2,1)S(1)}, bf16[1,64,128]{2,1,0:T(8,128)(2,1)S(1)}, u32[]{:S(2)}, u32[]{:S(2)}) %collective-permute-start.1) | collective-permute-done | bytes 16416 | tf_op jit(solution)/shard_map/ppermute | solution.py:104
  117.7 4.1 %collective-permute-done.2 = bf16[1,64,128]{2,1,0:T(8,128)(2,1)S(1)} collective-permute-done((bf16[1,64,128]{2,1,0:T(8,128)(2,1)S(1)}, bf16[1,64,128]{2,1,0:T(8,128)(2,1)S(1)}, u32[]{:S(2)}, u32[]{:S(2)}) %collective-permute-start.2) | collective-permute-done | bytes 16416 | tf_op jit(solution)/shard_map/ppermute | solution.py:104
  122.4 3.4 %fusion.1 = bf16[4096,128]{1,0:T(8,128)(2,1)} fusion(bf16[512,128]{1,0:T(8,128)(2,1)S(1)} %bitcast.96, s32[512]{0:T(512)S(1)} %eq.258), kind=kOutput, calls=%fused_computation.4 | convolution fusion | flops 539492352 | bytes 1181696 | tf_op jit(solution)/shard_map/dot_general | solution.py:20
  125.9 2.3 %fusion.3 = f32[1,1024]{1,0:T(1,128)S(1)} fusion(f32[1024,512]{1,0:T(8,128)} %get-tuple-element.27, f32[512]{0:T(512)S(1)} %bitcast.109, bf16[1,512]{1,0:T(2,128)(2,1)S(1)} %copy-done.3), kind=kOutput, calls=%fused_computation.23 | convolution fusion | flops 4194304 | bytes 2104320 | tf_op jit(solution)/shard_map/dot_general | solution.py:75
  128.2 14.1 %psum.28 = f32[1024]{0:T(1024)S(1)} all-reduce(f32[1024]{0:T(1024)S(1)} %bitcast.104), channel_id=1, replica_groups=mesh['dp'=4,'shard'=8] {'shard'}, use_global_device_ids=true, to_apply=%region_6.7 | all-reduce | flops 1024 | bytes 8192 | tf_op jit(solution)/shard_map/psum | solution.py:76
  142.9 2.3 %fusion.6 = f32[4096,128]{1,0:T(8,128)S(1)} fusion(s32[128]{0:T(128)S(1)} %get-tuple-element.24, s32[128]{0:T(128)S(1)} %get-tuple-element.25, s32[128]{0:T(128)S(1)} %get-tuple-element.19, s32[128]{0:T(128)S(1)} %get-tuple-element.20, s32[128]{0:T(128)S(1)} %get-tuple-element.21, s32[128]{0:T(128)S(1)} %get-tuple-element.22, ...), kind=kOutput, calls=%fused_computation.29 | convolution fusion | flops 146800640 | bytes 2134016 | tf_op jit(solution)/shard_map/dot_general | solution.py:20
  145.2 62.8 %all-reduce.5 = bf16[4096,128]{1,0:T(8,128)(2,1)} all-reduce(f32[4096,128]{1,0:T(8,128)S(1)} %fusion.6), channel_id=1, replica_groups=mesh['dp'=4,'shard'=8] {'dp','shard'}, use_global_device_ids=true, to_apply=%region_8.9 | all-reduce | flops 524288 | bytes 3145728 | tf_op jit(solution)/shard_map/psum | solution.py:91
  208.1 1.6 dynamic-slice_convert_fusion
  209.6 1.8 convert_element_type.86
  211.4 2.3 %copy.34 = bf16[4096,128]{1,0:T(8,128)(2,1)} copy(bf16[4096,128]{1,0:T(8,128)(2,1)} %get-tuple-element.30) | data formatting | bytes 2097152
  (68 shorter events, 14.9 us)
Async XLA Ops:
  7.2 36.4 %copy-start = (bf16[4096,128]{1,0:T(8,128)(2,1)S(1)}, bf16[4096,128]{1,0:T(8,128)(2,1)}, u32[]{:S(2)}) copy-start(bf16[4096,128]{1,0:T(8,128)(2,1)} %param.13) | copy-start | bytes 3145732
  12.9 21.9 %all-to-all-start.1 = ((s32[8,1,64]{2,1,0:T(1,128)}), s32[8,1,64]{2,1,0:T(1,128)S(1)}, u32[]{:S(2)}, u32[]{:S(2)}) async-start(s32[8,1,64]{2,1,0:T(1,128)} %all_to_all.21), calls=%async_computation.1 | async-start | bytes 8192 | tf_op jit(solution)/shard_map/all_to_all | solution.py:60
  34.8 8.7 %all-to-all-start = ((s32[8,1,64]{2,1,0:T(1,128)}), s32[8,1,64]{2,1,0:T(1,128)S(1)}, u32[]{:S(2)}, u32[]{:S(2)}) async-start(s32[8,1,64]{2,1,0:T(1,128)} %all_to_all.19), calls=%async_computation | async-start | bytes 8192 | tf_op jit(solution)/shard_map/all_to_all | solution.py:61
  45.8 10.1 %all-to-all-start.2 = ((bf16[8,64,128]{2,1,0:T(8,128)(2,1)}), bf16[8,64,128]{2,1,0:T(8,128)(2,1)S(1)}, u32[]{:S(2)}, u32[]{:S(2)}) async-start(bf16[8,64,128]{2,1,0:T(8,128)(2,1)} %select_select_fusion), calls=%async_computation.2 | async-start | bytes 262144 | tf_op jit(solution)/shard_map/all_to_all | solution.py:64
  49.2 54.3 %reduce-scatter.2.cloned.1.call-start = ((), (), s32[]{:S(2)}) async-start(), calls=%async_computation.4 | async-start | bytes 589824 | tf_op jit(solution)/shard_map/reduce_scatter | solution.py:84
  49.2 21.1 %copy-start.1 = (bf16[256,512]{1,0:T(8,128)(2,1)S(1)}, bf16[256,512]{1,0:T(8,128)(2,1)}, u32[]{:S(2)}) copy-start(bf16[256,512]{1,0:T(8,128)(2,1)} %param.14) | copy-start | bytes 786436
  73.8 135.8 %all-reduce.4.cloned.1.call-start = ((), (), s32[]{:S(2)}) async-start(), calls=%async_computation.5 | async-start | bytes 2621440 | tf_op jit(solution)/shard_map/psum | solution.py:112
  104.7 7.4 %collective-permute-start = (bf16[1,64,128]{2,1,0:T(8,128)(2,1)S(1)}, bf16[1,64,128]{2,1,0:T(8,128)(2,1)S(1)}, u32[]{:S(2)}, u32[]{:S(2)}) collective-permute-start(bf16[1,64,128]{2,1,0:T(8,128)(2,1)S(1)} %get-tuple-element.16), channel_id=1, source_target_pairs={{0,1},{1,2},{2,3},{3,4},{4,5},{5,6},{6,7},{7,0},{8,9},{9,10},{10,1... | collective-permute-start | bytes 49160 | tf_op jit(solution)/shard_map/ppermute | solution.py:104
  105.9 15.9 %collective-permute-start.6 = (bf16[1,64,128]{2,1,0:T(8,128)(2,1)S(1)}, bf16[1,64,128]{2,1,0:T(8,128)(2,1)S(1)}, u32[]{:S(2)}, u32[]{:S(2)}) collective-permute-start(bf16[1,64,128]{2,1,0:T(8,128)(2,1)S(1)} %get-tuple-element.10), channel_id=1, source_target_pairs={{0,7},{1,0},{2,1},{3,2},{4,3},{5,4},{6,5},{7,6},{8,15},{9,8},{10,9... | collective-permute-start | bytes 49160 | tf_op jit(solution)/shard_map/ppermute | solution.py:104
  109.4 12.3 %collective-permute-start.5 = (bf16[1,64,128]{2,1,0:T(8,128)(2,1)S(1)}, bf16[1,64,128]{2,1,0:T(8,128)(2,1)S(1)}, u32[]{:S(2)}, u32[]{:S(2)}) collective-permute-start(bf16[1,64,128]{2,1,0:T(8,128)(2,1)S(1)} %get-tuple-element.11), channel_id=1, source_target_pairs={{0,6},{1,7},{2,0},{3,1},{4,2},{5,3},{6,4},{7,5},{8,14},{9,15},{10,... | collective-permute-start | bytes 49160 | tf_op jit(solution)/shard_map/ppermute | solution.py:104
  109.5 12.3 %collective-permute-start.4 = (bf16[1,64,128]{2,1,0:T(8,128)(2,1)S(1)}, bf16[1,64,128]{2,1,0:T(8,128)(2,1)S(1)}, u32[]{:S(2)}, u32[]{:S(2)}) collective-permute-start(bf16[1,64,128]{2,1,0:T(8,128)(2,1)S(1)} %get-tuple-element.12), channel_id=1, source_target_pairs={{0,5},{1,6},{2,7},{3,0},{4,1},{5,2},{6,3},{7,4},{8,13},{9,14},{10,... | collective-permute-start | bytes 49160 | tf_op jit(solution)/shard_map/ppermute | solution.py:104
  109.5 12.3 %collective-permute-start.3 = (bf16[1,64,128]{2,1,0:T(8,128)(2,1)S(1)}, bf16[1,64,128]{2,1,0:T(8,128)(2,1)S(1)}, u32[]{:S(2)}, u32[]{:S(2)}) collective-permute-start(bf16[1,64,128]{2,1,0:T(8,128)(2,1)S(1)} %get-tuple-element.13), channel_id=1, source_target_pairs={{0,4},{1,5},{2,6},{3,7},{4,0},{5,1},{6,2},{7,3},{8,12},{9,13},{10,... | collective-permute-start | bytes 49160 | tf_op jit(solution)/shard_map/ppermute | solution.py:104
  112.1 5.5 %collective-permute-start.1 = (bf16[1,64,128]{2,1,0:T(8,128)(2,1)S(1)}, bf16[1,64,128]{2,1,0:T(8,128)(2,1)S(1)}, u32[]{:S(2)}, u32[]{:S(2)}) collective-permute-start(bf16[1,64,128]{2,1,0:T(8,128)(2,1)S(1)} %get-tuple-element.15), channel_id=1, source_target_pairs={{0,2},{1,3},{2,4},{3,5},{4,6},{5,7},{6,0},{7,1},{8,10},{9,11},{10,... | collective-permute-start | bytes 49160 | tf_op jit(solution)/shard_map/ppermute | solution.py:104
  117.7 4.1 %collective-permute-start.2 = (bf16[1,64,128]{2,1,0:T(8,128)(2,1)S(1)}, bf16[1,64,128]{2,1,0:T(8,128)(2,1)S(1)}, u32[]{:S(2)}, u32[]{:S(2)}) collective-permute-start(bf16[1,64,128]{2,1,0:T(8,128)(2,1)S(1)} %get-tuple-element.14), channel_id=1, source_target_pairs={{0,3},{1,4},{2,5},{3,6},{4,7},{5,0},{6,1},{7,2},{8,11},{9,12},{10,... | collective-permute-start | bytes 49160 | tf_op jit(solution)/shard_map/ppermute | solution.py:104
  122.4 3.5 %copy-start.3 = (bf16[1,512]{1,0:T(2,128)(2,1)S(1)}, bf16[1,512]{1,0:T(2,128)(2,1)}, u32[]{:S(2)}) copy-start(bf16[1,512]{1,0:T(2,128)(2,1)} %param.16) | copy-start | bytes 3076
  125.9 17.0 %copy-start.2 = (bf16[128,256]{1,0:T(8,128)(2,1)S(1)}, bf16[128,256]{1,0:T(8,128)(2,1)}, u32[]{:S(2)}) copy-start(bf16[128,256]{1,0:T(8,128)(2,1)} %reduce-scatter.2.cloned.1.call-done) | copy-start | bytes 196612
Sparse Core Ops, SparseCore 0:
  74.0 29.4 reduce-scatter.1
  126.0 58.5 all-reduce.3
